TPU v7x, 256 devices: a whole 4x4x8 slice. The times are simulated.
256 devices in a mesh: dom: 8 (over z), row: 16 (over y, x), col: 2 (over core).
Axes of the slice: x: 4, y: 4, z: 8, core: 2. Of those that a mesh axis runs over, the one named last changes fastest.
Arguments:
- next_inverse: bfloat16 [8, 4096, 4096], P('dom', 'row', 'col'), may hold values from -6 to 6
- next_arrow: bfloat16 [8, 64, 4096], P('dom', None, 'row'), may hold values from -6 to 6
- factor_win: bfloat16 [8, 4096, 3072], P('dom', 'row', 'col'), may hold values from -0.09375 to 0.09375
- factor_rest: bfloat16 [8, 4096, 1024], P('dom', 'row', 'col'), may hold values from -0.09375 to 0.09375
- arrow_win: bfloat16 [8, 64, 3072], P('dom', None, 'col'), may hold values from -0.75 to 0.75
- arrow_rest: bfloat16 [8, 64, 1024], P('dom', None, 'col'), may hold values from -0.75 to 0.75
- tip_inverse: bfloat16 [64, 64], replicated, may hold values from -6 to 6
- base_win: bfloat16 [8, 3072, 3072], P('dom', 'row', 'col'), may hold values from -6 to 6
- base_rest: bfloat16 [8, 3072, 1024], P('dom', 'row', 'col'), may hold values from -6 to 6
Outputs:
- sub_inverse: bfloat16 [8, 4096, 3072], P('dom', 'row', 'col')
- arrow_inverse: bfloat16 [8, 64, 3072], P('dom', None, 'col')
- diag_win: bfloat16 [8, 3072, 3072], P('dom', 'row', 'col')
- diag_rest: bfloat16 [8, 3072, 1024], P('dom', 'row', 'col')
All inputs are finite; a program needn't handle non-finite values.
Results may differ from a plain program's by a relative error of at most 0.0046.
Values may be sent and summed in bfloat16 or wider, within the bound.
A program may use at most 128 MiB of HBM per device.

v0:
```python
import jax
import jax.numpy as jnp
from jax import lax
from jax.sharding import PartitionSpec as P


def shifted(value, axis, steps):
    count = lax.axis_size(axis)
    leading, last = (max(0, -steps), min(count, count - steps))
    return lax.ppermute(value, axis, [(source, source + steps) for source in range(leading, last)])


def contract_first(left, right):
    return lax.dot_general(
        left, right, (((0,), (0,)), ((), ())), preferred_element_type=jnp.float32
    )


def per_device(
    next_inverse,
    next_arrow,
    factor_win,
    factor_rest,
    arrow_win,
    arrow_rest,
    tip_inverse,
    base_win,
    base_rest,
):
    inverse_tile = next_inverse[0]
    arrow_tile = next_arrow[0]
    factor_tile = factor_win[0]
    factor_other = factor_rest[0]
    ratio_tile = arrow_win[0]
    ratio_other = arrow_rest[0]
    factor_column = lax.all_gather(factor_tile, "row", axis=0, tiled=True)
    inverse_next, arrow_next = shifted((inverse_tile, arrow_tile), "dom", -1)
    start_sum = contract_first(arrow_next, ratio_tile)
    x_total = start_sum + jnp.dot(
        lax.all_gather(inverse_next, "col", axis=1, tiled=True),
        factor_column,
        preferred_element_type=jnp.float32,
    )
    x_bf = x_total.astype(jnp.bfloat16)
    y_part = jnp.dot(arrow_next, factor_tile, preferred_element_type=jnp.float32)
    y_total = lax.psum(y_part, "row") + jnp.dot(
        tip_inverse, ratio_tile, preferred_element_type=jnp.float32
    )
    y_bf = y_total.astype(jnp.bfloat16)
    x_panel, y_panel = (
        lax.all_gather(x_bf, "col", axis=1, tiled=True),
        lax.all_gather(y_bf, "col", axis=1, tiled=True),
    )
    ratio_both = jnp.concatenate([ratio_tile, ratio_other], axis=1)
    rows_here = y_panel.shape[1] // lax.axis_size("row")
    y_rows = lax.dynamic_slice_in_dim(y_panel, lax.axis_index("row") * rows_here, rows_here, 1)
    x_columns = lax.all_to_all(x_panel, "row", split_axis=1, concat_axis=0, tiled=True)
    rest_column = lax.all_gather(factor_other, "row", axis=0, tiled=True)
    factor_full = jnp.concatenate([factor_column, rest_column], axis=1)
    diag_part = contract_first(x_columns, factor_full)
    base_both = jnp.concatenate([base_win[0], base_rest[0]], axis=1).astype(jnp.float32)
    diag_total = base_both + diag_part + contract_first(y_rows, ratio_both)
    split = factor_tile.shape[1]
    diag_left = diag_total[:, :split].astype(jnp.bfloat16)
    diag_right = diag_total[:, split:].astype(jnp.bfloat16)
    return ((-x_bf)[None], (-y_bf)[None], diag_left[None], diag_right[None])


def solution(mesh):
    in_specs = (
        P("dom", "row", "col"),
        P("dom", None, "row"),
        P("dom", "row", "col"),
        P("dom", "row", "col"),
        P("dom", None, "col"),
        P("dom", None, "col"),
        P(),
        P("dom", "row", "col"),
        P("dom", "row", "col"),
    )
    out_specs = (
        P("dom", "row", "col"),
        P("dom", None, "col"),
        P("dom", "row", "col"),
        P("dom", "row", "col"),
    )
    return jax.shard_map(
        per_device, mesh=mesh, in_specs=in_specs, out_specs=out_specs, check_vma=False
    )
```

profile of v0, /device:TPU:1, one launch (start us, length us, event | category | flops | bytes accessed | tf_op | source)
XLA Modules:
  0.0 360.3 jit_solution(10407591954021950761)
XLA Ops:
  7.2 0.0 copy-start
  7.2 0.0 copy-start.7
  7.2 0.0 all-gather.7.cloned.1.call-start
  7.2 1.3 collective-permute-start.1
  8.5 24.2 %collective-permute-done.1 = bf16[256,2048]{1,0:T(8,128)(2,1)S(1)} collective-permute-done((bf16[256,2048]{1,0:T(8,128)(2,1)}, bf16[256,2048]{1,0:T(8,128)(2,1)S(1)}, u32[]{:S(2)}, u32[]{:S(2)}) %collective-permute-start.1) | collective-permute-done | bytes 1048608 | tf_op jit(solution)/shard_map/ppermute | solution.py:10
  32.8 0.0 copy-start.4
  32.8 1.0 copy-done.4
  33.8 0.0 all-gather.7.cloned.1.call-update
  33.8 0.0 all-gather.11.cloned.1.call-start
  33.9 0.7 all-gather.11.cloned.1.call-update
  34.6 0.0 all-gather.9.cloned.1.call-start
  34.6 0.0 copy-done.7
  34.6 0.0 copy-start.3
  34.6 1.4 collective-permute-start
  36.1 19.8 %all-gather.7.cloned.1.call-done = bf16[256,4096]{1,0:T(8,128)(2,1)} async-done(((bf16[256,2048]{1,0:T(8,128)(2,1)}), bf16[256,4096]{1,0:T(8,128)(2,1)}) %all-gather.7.cloned.1.call-update) | async-done | bytes 2097168 | tf_op jit(solution)/shard_map/all_gather | solution.py:40
  55.9 98.0 %all-gather.11.cloned.1.call-done = bf16[1,4096,1536]{2,1,0:T(8,128)(2,1)} async-done(((bf16[1,256,1536]{2,1,0:T(8,128)(2,1)}), bf16[1,4096,1536]{2,1,0:T(8,128)(2,1)}) %all-gather.11.cloned.1.call-update) | async-done | bytes 12582928 | tf_op jit(solution)/shard_map/all_gather | solution.py:36
  153.9 7.0 %fusion.18 = f32[256,1536]{1,0:T(8,128)S(1)} fusion(bf16[256,4096]{1,0:T(8,128)(2,1)} %all-gather.7.cloned.1.call-done, bf16[1,4096,1536]{2,1,0:T(8,128)(2,1)} %all-gather.11.cloned.1.call-done), kind=kOutput, calls=%fused_computation.23 | convolution fusion | flops 3221225472 | bytes 16252928 | tf_op jit(solution)/shard_map/dot_general | solution.py:39
  160.9 0.0 copy-start.2
  160.9 0.0 collective-permute-done
  161.0 0.0 copy-done.3
  161.0 1.3 fusion.4
  162.2 0.0 all-gather.9.cloned.1.call-update
  162.3 0.0 all-reduce.2.cloned.1.call-start
  162.3 0.0 copy-done.2
  162.3 1.0 fusion.9
  163.3 0.0 all-reduce.2.cloned.1.call-update
  163.3 0.0 all-gather.13.cloned.1.call-start
  163.4 0.5 all-gather.13.cloned.1.call-update
  163.9 14.1 %all-gather.9.cloned.1.call-done = bf16[256,3072]{1,0:T(8,128)(2,1)} async-done(((bf16[256,1536]{1,0:T(8,128)(2,1)}), bf16[256,3072]{1,0:T(8,128)(2,1)}) %all-gather.9.cloned.1.call-update) | async-done | bytes 1572880 | tf_op jit(solution)/shard_map/all_gather | solution.py:51
  178.0 2.6 copy.13
  180.6 6.3 %all-to-all-start = ((bf16[256,16,192]{0,2,1:T(8,128)(2,1)}), bf16[256,16,192]{0,2,1:T(8,128)(2,1)S(1)}, u32[]{:S(2)}, u32[]{:S(2)}) async-start(bf16[256,16,192]{0,2,1:T(8,128)(2,1)} %bitcast.9), calls=%async_computation | async-start | bytes 3145728 | tf_op jit(solution)/shard_map/all_to_all | solution.py:57
  186.9 0.0 copy-start.1
  186.9 0.0 copy-done
  186.9 0.2 fusion.20
  187.1 95.9 %all-reduce.2.cloned.1.call-done = f32[64,1536]{1,0:T(8,128)} async-done(((f32[64,1536]{1,0:T(8,128)}), f32[64,1536]{1,0:T(8,128)}) %all-reduce.2.cloned.1.call-update) | async-done | bytes 393232 | tf_op jit(solution)/shard_map/psum | solution.py:46
  283.0 1.7 negate_bitcast_fusion.1
  284.7 3.8 %all_gather.19 = bf16[64,3072]{1,0:T(8,128)(2,1)} all-gather(bf16[64,1536]{1,0:T(8,128)(2,1)S(1)} %get-tuple-element.5), channel_id=1, replica_groups=mesh['dom'=8,'row'=16,'col'=2] {'col'}, dimensions={1}, use_global_device_ids=true | all-gather | bytes 589824 | tf_op jit(solution)/shard_map/all_gather | solution.py:52
  288.5 0.0 copy-done.1
  288.5 0.9 negate_bitcast_fusion
  289.4 0.0 all-to-all-done
  289.4 0.2 copy.15
  289.6 53.0 %all-gather.13.cloned.1.call-done = bf16[1,4096,512]{2,1,0:T(8,128)(2,1)} async-done(((bf16[1,256,512]{2,1,0:T(8,128)(2,1)}), bf16[1,4096,512]{2,1,0:T(8,128)(2,1)}) %all-gather.13.cloned.1.call-update) | async-done | bytes 4194320 | tf_op jit(solution)/shard_map/all_gather | solution.py:58
  342.6 0.0 copy-done.6
  342.6 8.4 %fusion.5 = f32[192,2048]{1,0:T(8,128)S(1)} fusion(bf16[4096,192]{0,1:T(8,128)(2,1)S(1)} %bitcast.36, bf16[4096,512]{1,0:T(8,128)(2,1)} %bitcast.39, bf16[4096,1536]{1,0:T(8,128)(2,1)} %bitcast.38, bf16[192,512]{1,0:T(8,128)(2,1)S(1)} %bitcast.42, bf16[192,1536]{1,0:T(8,128)(2,1)} %bitcast.41), kind=kOutput, calls=%fused_computation.7 | convolution fusion | flops 3256745984 | bytes 20709376 | tf_op jit(solution)/shard_map/dot_general | solution.py:14
  350.9 0.0 copy-done.5
  351.0 1.3 fusion.8
  352.2 0.9 slice_bitcast_fusion
  353.1 0.7 slice_bitcast_fusion.1
  (2 shorter events, 0.0 us)
Async XLA Ops:
  7.2 179.7 %copy-start = (bf16[64,64]{1,0:T(8,128)(2,1)S(1)}, bf16[64,64]{1,0:T(8,128)(2,1)}, u32[]{:S(2)}) copy-start(bf16[64,64]{1,0:T(8,128)(2,1)} %param.15) | copy-start | bytes 24580
  7.2 27.4 %copy-start.7 = (bf16[1,64,256]{2,1,0:T(8,128)(2,1)S(1)}, bf16[1,64,256]{2,1,0:T(8,128)(2,1)}, u32[]{:S(2)}) copy-start(bf16[1,64,256]{2,1,0:T(8,128)(2,1)} %param.10) | copy-start | bytes 98308
  7.2 48.7 %all-gather.7.cloned.1.call-start = ((), (), s32[]{:S(2)}) async-start(), calls=%async_computation.1 | async-start | bytes 3145728 | tf_op jit(solution)/shard_map/all_gather | solution.py:40
  7.2 25.5 %collective-permute-start.1 = (bf16[256,2048]{1,0:T(8,128)(2,1)}, bf16[256,2048]{1,0:T(8,128)(2,1)S(1)}, u32[]{:S(2)}, u32[]{:S(2)}) collective-permute-start(bf16[256,2048]{1,0:T(8,128)(2,1)} %bitcast.40), channel_id=1, source_target_pairs={{32,0},{64,32},{96,64},{128,96},{160,128},{192,160},{224,192},{33,... | collective-permute-start | bytes 3145736 | tf_op jit(solution)/shard_map/ppermute | solution.py:10
  32.8 1.0 copy-start.4
  33.8 120.1 %all-gather.11.cloned.1.call-start = ((), (), s32[]{:S(2)}) async-start(), calls=%async_computation.4 | async-start | bytes 13369344 | tf_op jit(solution)/shard_map/all_gather | solution.py:36
  34.6 143.5 %all-gather.9.cloned.1.call-start = ((), (), s32[]{:S(2)}) async-start(), calls=%async_computation.3 | async-start | bytes 2359296 | tf_op jit(solution)/shard_map/all_gather | solution.py:51
  34.6 126.3 %copy-start.3 = (bf16[1,64,1536]{2,1,0:T(8,128)(2,1)S(1)}, bf16[1,64,1536]{2,1,0:T(8,128)(2,1)}, u32[]{:S(2)}) copy-start(bf16[1,64,1536]{2,1,0:T(8,128)(2,1)} %param.13) | copy-start | bytes 589828
  34.6 126.3 %collective-permute-start = (bf16[64,256]{1,0:T(8,128)(2,1)S(1)}, bf16[64,256]{1,0:T(8,128)(2,1)S(1)}, u32[]{:S(2)}, u32[]{:S(2)}) collective-permute-start(bf16[64,256]{1,0:T(8,128)(2,1)S(1)} %bitcast.43), channel_id=1, source_target_pairs={{32,0},{64,32},{96,64},{128,96},{160,128},{192,160},{224,192},{33,... | collective-permute-start | bytes 98312 | tf_op jit(solution)/shard_map/ppermute | solution.py:10
  160.9 1.4 copy-start.2
  162.3 120.7 %all-reduce.2.cloned.1.call-start = ((), (), s32[]{:S(2)}) async-start(), calls=%async_computation.2 | async-start | bytes 786432 | tf_op jit(solution)/shard_map/psum | solution.py:46
  163.3 179.2 %all-gather.13.cloned.1.call-start = ((), (), s32[]{:S(2)}) async-start(), calls=%async_computation.5 | async-start | bytes 4456448 | tf_op jit(solution)/shard_map/all_gather | solution.py:58
  180.6 108.8 %all-to-all-start = ((bf16[256,16,192]{0,2,1:T(8,128)(2,1)}), bf16[256,16,192]{0,2,1:T(8,128)(2,1)S(1)}, u32[]{:S(2)}, u32[]{:S(2)}) async-start(bf16[256,16,192]{0,2,1:T(8,128)(2,1)} %bitcast.9), calls=%async_computation | async-start | bytes 3145728 | tf_op jit(solution)/shard_map/all_to_all | solution.py:57
  186.9 101.6 %copy-start.1 = (bf16[256,1536]{1,0:T(8,128)(2,1)S(1)}, bf16[256,1536]{1,0:T(8,128)(2,1)}, u32[]{:S(2)}) copy-start(bf16[256,1536]{1,0:T(8,128)(2,1)} %fusion.4) | copy-start | bytes 2359300
  289.4 53.1 %copy-start.6 = (bf16[1,192,512]{2,1,0:T(8,128)(2,1)S(1)}, bf16[1,192,512]{2,1,0:T(8,128)(2,1)}, u32[]{:S(2)}) copy-start(bf16[1,192,512]{2,1,0:T(8,128)(2,1)} %param.17) | copy-start | bytes 589828
  342.6 8.4 %copy-start.5 = (bf16[1,64,512]{2,1,0:T(8,128)(2,1)S(1)}, bf16[1,64,512]{2,1,0:T(8,128)(2,1)}, u32[]{:S(2)}) copy-start(bf16[1,64,512]{2,1,0:T(8,128)(2,1)} %param.14) | copy-start | bytes 196612
Sparse Core Ops, SparseCore 0:
  33.9 21.8 all-gather.6
  58.3 95.5 all-gather.10
  162.4 15.6 all-gather.8
  181.7 101.2 all-reduce.1
  285.3 57.2 all-gather.12
where the time goes:
time: 361 us; the launch traced here: 360 us
  waiting for transfers between devices  306 us (85%)
  matrix products  19.1 us (5%)
  between operations  13.9 us (4%)
  starting transfers between devices  9.18 us (3%)
  local copies, waits for them, and re-layouts  5.35 us (1%)
  blocking collectives  3.8 us (1%)
    all_gather x1, waiting for transfers between devices, per_device(): factor_column = lax.all_gather(factor_tile, 'row', axis=0, tiled=True)  98 us
    psum x1, waiting for transfers between devices, per_device(): lax.psum(y_part, 'row')  95.9 us
    all_gather x1, waiting for transfers between devices, per_device(): rest_column = lax.all_gather(factor_other, 'row', axis=0, tiled=True)  53 us
    ppermute x2, waiting for transfers between devices, shifted(): lax.ppermute(value, axis, [(source, source + steps) for source in range(l...  24.2 us
    all_gather x1, waiting for transfers between devices, per_device(): lax.all_gather(inverse_next, 'col', axis=1, tiled=True)  19.8 us
    all_gather x1, waiting for transfers between devices, per_device(): lax.all_gather(x_bf, 'col', axis=1, tiled=True)  14.1 us
    dot_general x3, matrix products, contract_first(): lax.dot_general(left, right, (((0,), (0,)), ((), ())), preferred_element_...  10.9 us
  transfers between devices with their start and end apart: 8, of which 6 were waited for; matrix products, arithmetic and copies ran while one was open for 4% of the time, Pallas kernels for 0%

commit v1 on v0

--- a/solution.py
+++ b/solution.py
@@ -2,6 +2,27 @@
 import jax.numpy as jnp
 from jax import lax
 from jax.sharding import PartitionSpec as P
+
+
+def gather_around(value, axis, dim):
+    size, index, rows = (lax.axis_size(axis), lax.axis_index(axis), value.shape[dim])
+    forward = [(i, (i + 1) % size) for i in range(size)]
+    left = [(i, (i - 1) % size) for i in range(size)]
+    out = jnp.zeros((*value.shape[:dim], size * rows, *value.shape[dim + 1 :]), value.dtype)
+    out = lax.dynamic_update_slice_in_dim(out, value, index * rows, axis=dim)
+    from_left = from_right = value
+    halfway = size // 2
+    for turn in range(1, halfway + 1):
+        from_left = lax.ppermute(from_left, axis, forward)
+        out = lax.dynamic_update_slice_in_dim(
+            out, from_left, (index - turn) % size * rows, axis=dim
+        )
+        if turn < size - halfway:
+            from_right = lax.ppermute(from_right, axis, left)
+            out = lax.dynamic_update_slice_in_dim(
+                out, from_right, (index + turn) % size * rows, axis=dim
+            )
+    return out
 
 
 def shifted(value, axis, steps):
@@ -55,7 +76,7 @@
     rows_here = y_panel.shape[1] // lax.axis_size("row")
     y_rows = lax.dynamic_slice_in_dim(y_panel, lax.axis_index("row") * rows_here, rows_here, 1)
     x_columns = lax.all_to_all(x_panel, "row", split_axis=1, concat_axis=0, tiled=True)
-    rest_column = lax.all_gather(factor_other, "row", axis=0, tiled=True)
+    rest_column = gather_around(factor_other, "row", 0)
     factor_full = jnp.concatenate([factor_column, rest_column], axis=1)
     diag_part = contract_first(x_columns, factor_full)
     base_both = jnp.concatenate([base_win[0], base_rest[0]], axis=1).astype(jnp.float32)

time: 361 us -> 342 us (0.947)
  waiting for transfers between devices: 306 us -> 237 us
  starting transfers between devices: 9.18 us -> 41.6 us
  local copies, waits for them, and re-layouts: 5.35 us -> 20 us
    all_gather x1 -> x0, waiting for transfers between devices: 53 us -> none  [per_device(): rest_column = lax.all_gather(factor_other, 'row', axis=0, tiled=True)]
    ppermute x0 -> x15, starting transfers between devices: none -> 32.6 us  [the longest x7 29.5 us: gather_around(): from_right = lax.ppermute(from_right, axis, left)]
    ppermute x0 -> x15, waiting for transfers between devices: none -> 30.3 us  [the longest x7 18.7 us: gather_around(): from_right = lax.ppermute(from_right, axis, left)]
    all_gather x1, waiting for transfers between devices: 19.8 us -> 0.07 us  [per_device(): lax.all_gather(inverse_next, 'col', axis=1, tiled=True)]
    all_gather x1, waiting for transfers between devices: 14.1 us -> 0.01 us  [per_device(): lax.all_gather(x_bf, 'col', axis=1, tiled=True)]
    psum x1, waiting for transfers between devices: 95.9 us -> 83.3 us  [per_device(): lax.psum(y_part, 'row')]
    dynamic_update_slice x0 -> x16, local copies, waits for them, and re-layouts: none -> 12.5 us  [the longest x8 6.69 us: gather_around(): lax.dynamic_update_slice_in_dim(out, from_left, (index - turn) % size * r...]
  transfers between devices with their start and end apart: 8 -> 22, of which waited for: 6 -> 11; matrix products, arithmetic and copies ran while one was open for 4% -> 10% of each run, Pallas kernels for 0% -> 0%
where the time goes in v1:
time: 342 us; the launch traced here: 341 us
  waiting for transfers between devices  237 us (69%)
  starting transfers between devices  41.6 us (12%)
  matrix products  22 us (6%)
  local copies, waits for them, and re-layouts  20 us (6%)
  between operations  13.9 us (4%)
  blocking collectives  3.67 us (1%)
    all_gather x1, waiting for transfers between devices, per_device(): factor_column = lax.all_gather(factor_tile, 'row', axis=0, tiled=True)  98 us
    psum x1, waiting for transfers between devices, per_device(): lax.psum(y_part, 'row')  83.3 us
    ppermute x7, starting transfers between devices, gather_around(): from_right = lax.ppermute(from_right, axis, left)  29.5 us
    ppermute x2, waiting for transfers between devices, shifted(): lax.ppermute(value, axis, [(source, source + steps) for source in range(l...  24.2 us
    ppermute x7, waiting for transfers between devices, gather_around(): from_right = lax.ppermute(from_right, axis, left)  18.7 us
    dot_general x3, matrix products, contract_first(): lax.dot_general(left, right, (((0,), (0,)), ((), ())), preferred_element_...  11.7 us
    ppermute x8, waiting for transfers between devices, gather_around(): from_left = lax.ppermute(from_left, axis, forward)  11.5 us
    dot_general x1, matrix products, per_device(): jnp.dot(lax.all_gather(inverse_next, 'col', axis=1, tiled=True), factor_c...  7.05 us
  transfers between devices with their start and end apart: 22, of which 11 were waited for; matrix products, arithmetic and copies ran while one was open for 10% of the time, Pallas kernels for 0%

profile of v1, /device:TPU:1, one launch (start us, length us, event | category | flops | bytes accessed | tf_op | source)
XLA Modules:
  0.0 340.5 jit_solution(9944222487709581829)
XLA Ops:
  7.2 1.3 collective-permute-start.1
  8.5 24.2 %collective-permute-done.1 = bf16[256,2048]{1,0:T(8,128)(2,1)S(1)} collective-permute-done((bf16[256,2048]{1,0:T(8,128)(2,1)}, bf16[256,2048]{1,0:T(8,128)(2,1)S(1)}, u32[]{:S(2)}, u32[]{:S(2)}) %collective-permute-start.1) | collective-permute-done | bytes 1048608 | tf_op jit(solution)/shard_map/ppermute | solution.py:31
  32.8 1.0 copy-done.3
  34.6 3.1 collective-permute-start.2
  37.7 3.8 %collective-permute-start.3 = (bf16[256,512]{1,0:T(8,128)(2,1)}, bf16[256,512]{1,0:T(8,128)(2,1)S(1)}, u32[]{:S(2)}, u32[]{:S(2)}) collective-permute-start(bf16[256,512]{1,0:T(8,128)(2,1)} %bitcast.40), channel_id=1, source_target_pairs={{0,30},{2,0},{4,2},{6,4},{8,6},{10,8},{12,10},{14,12},{16,14},{18,... | collective-permute-start | bytes 786440 | tf_op jit(solution)/shard_map/ppermute | solution.py:21
  41.5 1.3 collective-permute-start
  42.8 4.0 %collective-permute-done.2 = bf16[256,512]{1,0:T(8,128)(2,1)S(1)} collective-permute-done((bf16[256,512]{1,0:T(8,128)(2,1)}, bf16[256,512]{1,0:T(8,128)(2,1)S(1)}, u32[]{:S(2)}, u32[]{:S(2)}) %collective-permute-start.2) | collective-permute-done | bytes 262176 | tf_op jit(solution)/shard_map/ppermute | solution.py:16
  46.8 1.1 fusion.26
  47.9 2.1 fusion.14
  50.1 4.9 %collective-permute-start.5 = (bf16[256,512]{1,0:T(8,128)(2,1)S(1)}, bf16[256,512]{1,0:T(8,128)(2,1)S(1)}, u32[]{:S(2)}, u32[]{:S(2)}) collective-permute-start(bf16[256,512]{1,0:T(8,128)(2,1)S(1)} %collective-permute-done.3), channel_id=1, source_target_pairs={{0,30},{2,0},{4,2},{6,4},{8,6},{10,8},{12,10},{14,12},{16,14},{18,... | collective-permute-start | bytes 786440 | tf_op jit(solution)/shard_map/ppermute | solution.py:21
  55.0 0.8 collective-permute-done.4
  55.9 98.0 %all-gather.9.cloned.1.call-done = bf16[1,4096,1536]{2,1,0:T(8,128)(2,1)} async-done(((bf16[1,256,1536]{2,1,0:T(8,128)(2,1)}), bf16[1,4096,1536]{2,1,0:T(8,128)(2,1)}) %all-gather.9.cloned.1.call-update) | async-done | bytes 12582928 | tf_op jit(solution)/shard_map/all_gather | solution.py:57
  153.9 7.1 %fusion.24 = f32[256,1536]{1,0:T(8,128)S(1)} fusion(bf16[256,4096]{1,0:T(8,128)(2,1)} %all-gather.5.cloned.1.call-done, bf16[1,4096,1536]{2,1,0:T(8,128)(2,1)} %all-gather.9.cloned.1.call-done), kind=kOutput, calls=%fused_computation.40 | convolution fusion | flops 3221225472 | bytes 16252928 | tf_op jit(solution)/shard_map/dot_general | solution.py:60
  161.0 1.3 fusion.4
  162.3 2.2 broadcast_in_dim.17
  164.5 0.7 constant_dynamic-update-slice_fusion.15
  165.2 0.7 constant_dynamic-update-slice_fusion.14
  165.9 0.7 constant_dynamic-update-slice_fusion.13
  166.7 2.7 collective-permute-start.7
  169.4 83.3 %all-reduce.2.cloned.1.call-done = f32[64,1536]{1,0:T(8,128)} async-done(((f32[64,1536]{1,0:T(8,128)}), f32[64,1536]{1,0:T(8,128)}) %all-reduce.2.cloned.1.call-update) | async-done | bytes 393232 | tf_op jit(solution)/shard_map/psum | solution.py:67
  252.7 1.7 negate_bitcast_fusion.1
  254.4 3.7 %all_gather.15 = bf16[64,3072]{1,0:T(8,128)(2,1)S(1)} all-gather(bf16[64,1536]{1,0:T(8,128)(2,1)S(1)} %get-tuple-element.5), channel_id=1, replica_groups=mesh['dom'=8,'row'=16,'col'=2] {'col'}, dimensions={1}, use_global_device_ids=true | all-gather | bytes 589824 | tf_op jit(solution)/shard_map/all_gather | solution.py:73
  258.0 2.4 collective-permute-start.9
  260.5 1.6 fusion.16
  262.1 0.7 constant_dynamic-update-slice_fusion.12
  262.8 0.7 constant_dynamic-update-slice_fusion.11
  263.5 2.3 collective-permute-done.9
  265.8 5.5 %collective-permute-start.11 = (bf16[256,512]{1,0:T(8,128)(2,1)S(1)}, bf16[256,512]{1,0:T(8,128)(2,1)S(1)}, u32[]{:S(2)}, u32[]{:S(2)}) collective-permute-start(bf16[256,512]{1,0:T(8,128)(2,1)S(1)} %collective-permute-done.9), channel_id=1, source_target_pairs={{0,30},{2,0},{4,2},{6,4},{8,6},{10,8},{12,10},{14,12},{16,14},{18,... | collective-permute-start | bytes 786440 | tf_op jit(solution)/shard_map/ppermute | solution.py:21
  271.3 0.7 constant_dynamic-update-slice_fusion.10
  272.6 0.7 constant_dynamic-update-slice_fusion.9
  273.3 2.6 copy.13
  275.9 6.3 %all-to-all-start = ((bf16[256,16,192]{0,2,1:T(8,128)(2,1)}), bf16[256,16,192]{0,2,1:T(8,128)(2,1)S(1)}, u32[]{:S(2)}, u32[]{:S(2)}) async-start(bf16[256,16,192]{0,2,1:T(8,128)(2,1)} %bitcast.36), calls=%async_computation | async-start | bytes 3145728 | tf_op jit(solution)/shard_map/all_to_all | solution.py:78
  282.2 0.7 constant_dynamic-update-slice_fusion.8
  282.9 4.7 %collective-permute-start.13 = (bf16[256,512]{1,0:T(8,128)(2,1)S(1)}, bf16[256,512]{1,0:T(8,128)(2,1)S(1)}, u32[]{:S(2)}, u32[]{:S(2)}) collective-permute-start(bf16[256,512]{1,0:T(8,128)(2,1)S(1)} %collective-permute-done.11), channel_id=1, source_target_pairs={{0,30},{2,0},{4,2},{6,4},{8,6},{10,8},{12,10},{14,12},{16,14},{18,... | collective-permute-start | bytes 786440 | tf_op jit(solution)/shard_map/ppermute | solution.py:21
  287.6 0.7 constant_dynamic-update-slice_fusion.7
  288.3 0.7 constant_dynamic-update-slice_fusion.6
  289.1 0.7 constant_dynamic-update-slice_fusion.5
  289.8 15.8 %collective-permute-done.13 = bf16[256,512]{1,0:T(8,128)(2,1)S(1)} collective-permute-done((bf16[256,512]{1,0:T(8,128)(2,1)S(1)}, bf16[256,512]{1,0:T(8,128)(2,1)S(1)}, u32[]{:S(2)}, u32[]{:S(2)}) %collective-permute-start.13) | collective-permute-done | bytes 262176 | tf_op jit(solution)/shard_map/ppermute | solution.py:21
  305.6 5.5 %collective-permute-start.15 = (bf16[256,512]{1,0:T(8,128)(2,1)S(1)}, bf16[256,512]{1,0:T(8,128)(2,1)S(1)}, u32[]{:S(2)}, u32[]{:S(2)}) collective-permute-start(bf16[256,512]{1,0:T(8,128)(2,1)S(1)} %collective-permute-done.13), channel_id=1, source_target_pairs={{0,30},{2,0},{4,2},{6,4},{8,6},{10,8},{12,10},{14,12},{16,14},{18,... | collective-permute-start | bytes 786440 | tf_op jit(solution)/shard_map/ppermute | solution.py:21
  311.1 1.7 constant_dynamic-update-slice_fusion.4
  312.8 0.8 constant_dynamic-update-slice_fusion.3
  313.5 0.7 constant_dynamic-update-slice_fusion.2
  314.9 0.7 constant_dynamic-update-slice_fusion.1
  315.6 6.2 %collective-permute-done.16 = bf16[256,512]{1,0:T(8,128)(2,1)S(1)} collective-permute-done((bf16[256,512]{1,0:T(8,128)(2,1)S(1)}, bf16[256,512]{1,0:T(8,128)(2,1)S(1)}, u32[]{:S(2)}, u32[]{:S(2)}) %collective-permute-start.16) | collective-permute-done | bytes 262176 | tf_op jit(solution)/shard_map/ppermute | solution.py:16
  321.8 0.7 constant_dynamic-update-slice_fusion
  322.6 0.9 negate_bitcast_fusion
  323.7 8.8 %fusion.11 = bf16[192,2048]{1,0:T(8,128)(2,1)S(1)} fusion(f32[192,2048]{1,0:T(8,128)} %fusion.16, bf16[4096,192]{0,1:T(8,128)(2,1)S(1)} %bitcast.38, bf16[4096,512]{1,0:T(8,128)(2,1)} %constant_dynamic-update-slice_fusion, bf16[4096,1536]{1,0:T(8,128)(2,1)} %bitcast.42, bf16[192,512]{1,0:T(8,128)(2,1)S(1)} %bitcast.45, bf16[192,1536]{1,0:T(8,128)(2,1)} %bitcast.44), kind=kOutput, calls=%fused_computation.8 | convolution fusion | flops 3257532416 | bytes 21495808 | tf_op jit(solution)/shard_map/dot_general | solution.py:35
  332.5 0.9 slice_bitcast_fusion
  (44 shorter events, 3.2 us)
Async XLA Ops:
  7.2 39.6 %copy-start = (bf16[64,64]{1,0:T(8,128)(2,1)S(1)}, bf16[64,64]{1,0:T(8,128)(2,1)}, u32[]{:S(2)}) copy-start(bf16[64,64]{1,0:T(8,128)(2,1)} %param.15) | copy-start | bytes 24580
  7.2 48.7 %all-gather.5.cloned.1.call-start = ((), (), s32[]{:S(2)}) async-start(), calls=%async_computation.1 | async-start | bytes 3145728 | tf_op jit(solution)/shard_map/all_gather | solution.py:61
  7.2 25.5 %collective-permute-start.1 = (bf16[256,2048]{1,0:T(8,128)(2,1)}, bf16[256,2048]{1,0:T(8,128)(2,1)S(1)}, u32[]{:S(2)}, u32[]{:S(2)}) collective-permute-start(bf16[256,2048]{1,0:T(8,128)(2,1)} %bitcast.43), channel_id=1, source_target_pairs={{32,0},{64,32},{96,64},{128,96},{160,128},{192,160},{224,192},{33,... | collective-permute-start | bytes 3145736 | tf_op jit(solution)/shard_map/ppermute | solution.py:31
  32.8 1.0 copy-start.3
  33.8 120.1 %all-gather.9.cloned.1.call-start = ((), (), s32[]{:S(2)}) async-start(), calls=%async_computation.4 | async-start | bytes 13369344 | tf_op jit(solution)/shard_map/all_gather | solution.py:57
  34.5 218.1 %all-reduce.2.cloned.1.call-start = ((), (), s32[]{:S(2)}) async-start(), calls=%async_computation.2 | async-start | bytes 786432 | tf_op jit(solution)/shard_map/psum | solution.py:67
  34.6 12.2 %collective-permute-start.2 = (bf16[256,512]{1,0:T(8,128)(2,1)}, bf16[256,512]{1,0:T(8,128)(2,1)S(1)}, u32[]{:S(2)}, u32[]{:S(2)}) collective-permute-start(bf16[256,512]{1,0:T(8,128)(2,1)} %bitcast.39), channel_id=1, source_target_pairs={{0,2},{2,4},{4,6},{6,8},{8,10},{10,12},{12,14},{14,16},{16,18},{18... | collective-permute-start | bytes 786440 | tf_op jit(solution)/shard_map/ppermute | solution.py:16
  37.7 12.4 %collective-permute-start.3 = (bf16[256,512]{1,0:T(8,128)(2,1)}, bf16[256,512]{1,0:T(8,128)(2,1)S(1)}, u32[]{:S(2)}, u32[]{:S(2)}) collective-permute-start(bf16[256,512]{1,0:T(8,128)(2,1)} %bitcast.40), channel_id=1, source_target_pairs={{0,30},{2,0},{4,2},{6,4},{8,6},{10,8},{12,10},{14,12},{16,14},{18,... | collective-permute-start | bytes 786440 | tf_op jit(solution)/shard_map/ppermute | solution.py:21
  41.5 6.4 %collective-permute-start = (bf16[64,256]{1,0:T(8,128)(2,1)}, bf16[64,256]{1,0:T(8,128)(2,1)S(1)}, u32[]{:S(2)}, u32[]{:S(2)}) collective-permute-start(bf16[64,256]{1,0:T(8,128)(2,1)} %bitcast.46), channel_id=1, source_target_pairs={{32,0},{64,32},{96,64},{128,96},{160,128},{192,160},{224,192},{33,... | collective-permute-start | bytes 98312 | tf_op jit(solution)/shard_map/ppermute | solution.py:31
  46.8 9.0 %collective-permute-start.4 = (bf16[256,512]{1,0:T(8,128)(2,1)S(1)}, bf16[256,512]{1,0:T(8,128)(2,1)S(1)}, u32[]{:S(2)}, u32[]{:S(2)}) collective-permute-start(bf16[256,512]{1,0:T(8,128)(2,1)S(1)} %collective-permute-done.2), channel_id=1, source_target_pairs={{0,2},{2,4},{4,6},{6,8},{8,10},{10,12},{12,14},{14,16},{16,18},{18... | collective-permute-start | bytes 786440 | tf_op jit(solution)/shard_map/ppermute | solution.py:16
  50.1 110.9 %copy-start.2 = (bf16[1,64,1536]{2,1,0:T(8,128)(2,1)S(1)}, bf16[1,64,1536]{2,1,0:T(8,128)(2,1)}, u32[]{:S(2)}) copy-start(bf16[1,64,1536]{2,1,0:T(8,128)(2,1)} %param.13) | copy-start | bytes 589828
  50.1 223.3 %all-gather.7.cloned.1.call-start = ((), (), s32[]{:S(2)}) async-start(), calls=%async_computation.3 | async-start | bytes 2359296 | tf_op jit(solution)/shard_map/all_gather | solution.py:72
  50.1 116.6 %collective-permute-start.5 = (bf16[256,512]{1,0:T(8,128)(2,1)S(1)}, bf16[256,512]{1,0:T(8,128)(2,1)S(1)}, u32[]{:S(2)}, u32[]{:S(2)}) collective-permute-start(bf16[256,512]{1,0:T(8,128)(2,1)S(1)} %collective-permute-done.3), channel_id=1, source_target_pairs={{0,30},{2,0},{4,2},{6,4},{8,6},{10,8},{12,10},{14,12},{16,14},{18,... | collective-permute-start | bytes 786440 | tf_op jit(solution)/shard_map/ppermute | solution.py:21
  55.8 113.6 %collective-permute-start.6 = (bf16[256,512]{1,0:T(8,128)(2,1)S(1)}, bf16[256,512]{1,0:T(8,128)(2,1)S(1)}, u32[]{:S(2)}, u32[]{:S(2)}) collective-permute-start(bf16[256,512]{1,0:T(8,128)(2,1)S(1)} %collective-permute-done.4), channel_id=1, source_target_pairs={{0,2},{2,4},{4,6},{6,8},{8,10},{10,12},{12,14},{14,16},{16,18},{18... | collective-permute-start | bytes 786440 | tf_op jit(solution)/shard_map/ppermute | solution.py:16
  161.0 3.5 %copy-start.4 = (bf16[1,256,512]{2,1,0:T(8,128)(2,1)S(1)}, bf16[1,256,512]{2,1,0:T(8,128)(2,1)}, u32[]{:S(2)}) copy-start(bf16[1,256,512]{2,1,0:T(8,128)(2,1)} %param.12) | copy-start | bytes 786436
  162.3 98.2 %copy-start.5 = (bf16[1,64,512]{2,1,0:T(8,128)(2,1)S(1)}, bf16[1,64,512]{2,1,0:T(8,128)(2,1)}, u32[]{:S(2)}) copy-start(bf16[1,64,512]{2,1,0:T(8,128)(2,1)} %param.14) | copy-start | bytes 196612
  166.7 91.4 %collective-permute-start.7 = (bf16[256,512]{1,0:T(8,128)(2,1)S(1)}, bf16[256,512]{1,0:T(8,128)(2,1)S(1)}, u32[]{:S(2)}, u32[]{:S(2)}) collective-permute-start(bf16[256,512]{1,0:T(8,128)(2,1)S(1)} %collective-permute-done.5), channel_id=1, source_target_pairs={{0,30},{2,0},{4,2},{6,4},{8,6},{10,8},{12,10},{14,12},{16,14},{18,... | collective-permute-start | bytes 786440 | tf_op jit(solution)/shard_map/ppermute | solution.py:21
  169.4 92.8 %collective-permute-start.8 = (bf16[256,512]{1,0:T(8,128)(2,1)S(1)}, bf16[256,512]{1,0:T(8,128)(2,1)S(1)}, u32[]{:S(2)}, u32[]{:S(2)}) collective-permute-start(bf16[256,512]{1,0:T(8,128)(2,1)S(1)} %collective-permute-done.6), channel_id=1, source_target_pairs={{0,2},{2,4},{4,6},{6,8},{8,10},{10,12},{12,14},{14,16},{16,18},{18... | collective-permute-start | bytes 786440 | tf_op jit(solution)/shard_map/ppermute | solution.py:16
  258.0 7.8 %collective-permute-start.9 = (bf16[256,512]{1,0:T(8,128)(2,1)S(1)}, bf16[256,512]{1,0:T(8,128)(2,1)S(1)}, u32[]{:S(2)}, u32[]{:S(2)}) collective-permute-start(bf16[256,512]{1,0:T(8,128)(2,1)S(1)} %collective-permute-done.7), channel_id=1, source_target_pairs={{0,30},{2,0},{4,2},{6,4},{8,6},{10,8},{12,10},{14,12},{16,14},{18,... | collective-permute-start | bytes 786440 | tf_op jit(solution)/shard_map/ppermute | solution.py:21
  262.1 10.5 %collective-permute-start.10 = (bf16[256,512]{1,0:T(8,128)(2,1)S(1)}, bf16[256,512]{1,0:T(8,128)(2,1)S(1)}, u32[]{:S(2)}, u32[]{:S(2)}) collective-permute-start(bf16[256,512]{1,0:T(8,128)(2,1)S(1)} %collective-permute-done.8), channel_id=1, source_target_pairs={{0,2},{2,4},{4,6},{6,8},{8,10},{10,12},{12,14},{14,16},{16,18},{18... | collective-permute-start | bytes 786440 | tf_op jit(solution)/shard_map/ppermute | solution.py:16
  265.8 17.1 %collective-permute-start.11 = (bf16[256,512]{1,0:T(8,128)(2,1)S(1)}, bf16[256,512]{1,0:T(8,128)(2,1)S(1)}, u32[]{:S(2)}, u32[]{:S(2)}) collective-permute-start(bf16[256,512]{1,0:T(8,128)(2,1)S(1)} %collective-permute-done.9), channel_id=1, source_target_pairs={{0,30},{2,0},{4,2},{6,4},{8,6},{10,8},{12,10},{14,12},{16,14},{18,... | collective-permute-start | bytes 786440 | tf_op jit(solution)/shard_map/ppermute | solution.py:21
  272.6 15.7 %collective-permute-start.12 = (bf16[256,512]{1,0:T(8,128)(2,1)S(1)}, bf16[256,512]{1,0:T(8,128)(2,1)}, u32[]{:S(2)}, u32[]{:S(2)}) collective-permute-start(bf16[256,512]{1,0:T(8,128)(2,1)S(1)} %collective-permute-done.10), channel_id=1, source_target_pairs={{0,2},{2,4},{4,6},{6,8},{8,10},{10,12},{12,14},{14,16},{16,18},{18... | collective-permute-start | bytes 786440 | tf_op jit(solution)/shard_map/ppermute | solution.py:16
  275.9 46.6 %copy-start.1 = (bf16[256,1536]{1,0:T(8,128)(2,1)S(1)}, bf16[256,1536]{1,0:T(8,128)(2,1)}, u32[]{:S(2)}) copy-start(bf16[256,1536]{1,0:T(8,128)(2,1)} %fusion.4) | copy-start | bytes 2359300
  275.9 47.6 %all-to-all-start = ((bf16[256,16,192]{0,2,1:T(8,128)(2,1)}), bf16[256,16,192]{0,2,1:T(8,128)(2,1)S(1)}, u32[]{:S(2)}, u32[]{:S(2)}) async-start(bf16[256,16,192]{0,2,1:T(8,128)(2,1)} %bitcast.36), calls=%async_computation | async-start | bytes 3145728 | tf_op jit(solution)/shard_map/all_to_all | solution.py:78
  282.9 22.6 %collective-permute-start.13 = (bf16[256,512]{1,0:T(8,128)(2,1)S(1)}, bf16[256,512]{1,0:T(8,128)(2,1)S(1)}, u32[]{:S(2)}, u32[]{:S(2)}) collective-permute-start(bf16[256,512]{1,0:T(8,128)(2,1)S(1)} %collective-permute-done.11), channel_id=1, source_target_pairs={{0,30},{2,0},{4,2},{6,4},{8,6},{10,8},{12,10},{14,12},{16,14},{18,... | collective-permute-start | bytes 786440 | tf_op jit(solution)/shard_map/ppermute | solution.py:21
  288.3 35.3 %copy-start.6 = (bf16[1,192,512]{2,1,0:T(8,128)(2,1)S(1)}, bf16[1,192,512]{2,1,0:T(8,128)(2,1)}, u32[]{:S(2)}) copy-start(bf16[1,192,512]{2,1,0:T(8,128)(2,1)} %param.17) | copy-start | bytes 589828
  288.3 24.4 %collective-permute-start.14 = (bf16[256,512]{1,0:T(8,128)(2,1)}, bf16[256,512]{1,0:T(8,128)(2,1)S(1)}, u32[]{:S(2)}, u32[]{:S(2)}) collective-permute-start(bf16[256,512]{1,0:T(8,128)(2,1)} %collective-permute-done.12), channel_id=1, source_target_pairs={{0,2},{2,4},{4,6},{6,8},{8,10},{10,12},{12,14},{14,16},{16,18},{18... | collective-permute-start | bytes 786440 | tf_op jit(solution)/shard_map/ppermute | solution.py:16
  305.6 9.4 %collective-permute-start.15 = (bf16[256,512]{1,0:T(8,128)(2,1)S(1)}, bf16[256,512]{1,0:T(8,128)(2,1)S(1)}, u32[]{:S(2)}, u32[]{:S(2)}) collective-permute-start(bf16[256,512]{1,0:T(8,128)(2,1)S(1)} %collective-permute-done.13), channel_id=1, source_target_pairs={{0,30},{2,0},{4,2},{6,4},{8,6},{10,8},{12,10},{14,12},{16,14},{18,... | collective-permute-start | bytes 786440 | tf_op jit(solution)/shard_map/ppermute | solution.py:21
  312.8 9.1 %collective-permute-start.16 = (bf16[256,512]{1,0:T(8,128)(2,1)S(1)}, bf16[256,512]{1,0:T(8,128)(2,1)S(1)}, u32[]{:S(2)}, u32[]{:S(2)}) collective-permute-start(bf16[256,512]{1,0:T(8,128)(2,1)S(1)} %collective-permute-done.14), channel_id=1, source_target_pairs={{0,2},{2,4},{4,6},{6,8},{8,10},{10,12},{12,14},{14,16},{16,18},{18... | collective-permute-start | bytes 786440 | tf_op jit(solution)/shard_map/ppermute | solution.py:16
Sparse Core Ops, SparseCore 0:
  33.9 21.8 all-gather.4
  58.3 95.5 all-gather.8
  157.7 94.9 all-reduce.1
  254.9 16.5 all-gather.6
